TPU v7x, 512 devices: a whole 4x4x16 slice. The times are simulated.
512 devices in a mesh: dp: 16 (over z), head: 8 (over x, core), srv: 4 (over y).
Axes of the slice: x: 4, y: 4, z: 16, core: 2. Of those that a mesh axis runs over, the one named last changes fastest.
Arguments:
- queries: bfloat16 [2048, 8, 1024], P('dp', 'srv', 'head'), may hold values from -5 to 5
- keys: bfloat16 [10240, 1024], P(('dp', 'head')), may hold values from -5 to 5
- values: bfloat16 [10240, 1024], P(('dp', 'head')), may hold values from -6 to 6
- output_gradient: bfloat16 [2048, 8, 1024], P('dp', 'srv', 'head'), may hold values from -6 to 6
- doc_ids: int32 [10240], P('dp'), may hold values from 0 to 7, never falling along the last dimension, each value on 1 to 5120 neighbouring positions
Outputs:
- attention: bfloat16 [2048, 8, 1024], P('dp', 'srv', 'head')
- q_grad: bfloat16 [2048, 8, 1024], P('dp', 'srv', 'head')
- k_grad: bfloat16 [10240, 1024], P(('dp', 'head', 'srv'))
- v_grad: bfloat16 [10240, 1024], P(('dp', 'head', 'srv'))
Inputs may be any that keep to these rules, and one draw needn't show every extreme that they name: `doc_ids`: document numbers never fall along the keys; every document holds at most 5120 keys, and one holds exactly 5120.
All inputs are finite; a program needn't handle non-finite values.
Results may differ from a plain program's by a relative error of at most 0.039.
Values may be sent and summed in bfloat16 or wider, within the bound.
No kernel may reach another device: no remote copies, remote signals or barrier semaphores. Data moves between devices by JAX's collectives and lax.ppermute only.
A program may use at most 64 MiB of HBM per device.

v0:
```python
import math
import jax
import jax.numpy as jnp
from jax import lax
from jax.sharding import PartitionSpec as P

HEAD_SIZE = 128
NEGATIVE = -1e30


def local(queries, keys, values, output_gradient, doc_ids):
    home_rows, pair_heads, group_width = queries.shape
    groups = group_width // HEAD_SIZE
    scale_factor = HEAD_SIZE ** (-0.5)
    key_rows, value_rows = (
        lax.all_to_all(keys, "head", split_axis=1, concat_axis=0, tiled=True),
        lax.all_to_all(values, "head", split_axis=1, concat_axis=0, tiled=True),
    )
    key_count = key_rows.shape[0]
    servers = lax.axis_size("dp")
    server = lax.axis_index("dp")
    key_at = server * key_count + jnp.arange(key_count, dtype=jnp.int32)
    all_docs = lax.all_gather(doc_ids, "dp", axis=0, tiled=True)
    query_total = home_rows * servers
    context = all_docs.shape[0] - query_total
    query_docs = all_docs[context:]
    query_places = context + jnp.arange(query_total, dtype=jnp.int32)
    all_q, all_dout = (
        lax.all_gather(queries, "dp", axis=0, tiled=True),
        lax.all_gather(output_gradient, "dp", axis=0, tiled=True),
    )
    block_rows = math.gcd(512, query_total)
    block_count = query_total // block_rows
    key_heads = key_rows.reshape(key_count, groups, HEAD_SIZE)
    value_heads = value_rows.reshape(key_count, groups, HEAD_SIZE)
    query_blocks = all_q.reshape(block_count, block_rows, pair_heads, groups, HEAD_SIZE)
    grad_blocks = all_dout.reshape(block_count, block_rows, pair_heads, groups, HEAD_SIZE)
    place_blocks = query_places.reshape(block_count, block_rows)
    doc_blocks = query_docs.reshape(block_count, block_rows)

    def admissible(places, query_doc):
        return (key_at[None, :] <= places[:, None]) & (doc_ids[None, :] == query_doc[:, None])

    def scores_of(query_block):
        return (
            jnp.einsum("pjgd,kgd->gjpk", query_block, key_heads, preferred_element_type=jnp.float32)
            * scale_factor
        )

    def block_max(inputs):
        query_block, places, query_doc = inputs
        allowed = admissible(places, query_doc)

        def compute():
            raw_scores = scores_of(query_block)
            masked = jnp.where(allowed[None, None], raw_scores, NEGATIVE)
            return (jnp.max(masked, axis=-1).transpose(2, 1, 0), raw_scores)

        return compute()

    def block_top(inputs):
        return block_max(inputs)[0]

    local_max = lax.map(block_top, (query_blocks, place_blocks, doc_blocks))
    row_max = lax.pmax(local_max.reshape(query_total, pair_heads, groups), "dp")
    max_blocks = row_max.reshape(block_count, block_rows, pair_heads, groups)

    def block_sum(inputs):
        stored, places, query_doc, row_top = inputs
        allowed = admissible(places, query_doc)

        def compute():
            block_scores = scores_of(stored)
            shifted = block_scores - row_top.transpose(2, 1, 0)[..., None]
            weights = jnp.where(allowed[None, None], jnp.exp(shifted), 0.0)
            weighted = jnp.einsum(
                "gjpk,kgd->pjgd",
                weights.astype(jnp.bfloat16),
                value_heads,
                preferred_element_type=jnp.float32,
            )
            return (
                weighted.reshape(block_rows, pair_heads, group_width),
                jnp.sum(weights, axis=-1).transpose(2, 1, 0),
            )

        return compute()

    part_out, part_norm = lax.map(block_sum, (query_blocks, place_blocks, doc_blocks, max_blocks))
    part_out = part_out.reshape(query_total, pair_heads, group_width)
    part_norm = part_norm.reshape(query_total, pair_heads, groups)
    home_out, home_norm = (
        lax.psum_scatter(part_out, "dp", scatter_dimension=0, tiled=True),
        lax.psum_scatter(part_norm, "dp", scatter_dimension=0, tiled=True),
    )
    home_max = lax.dynamic_slice_in_dim(row_max, server * home_rows, home_rows, 0)
    attn_home = (
        home_out.reshape(home_rows, pair_heads, groups, HEAD_SIZE) / home_norm[..., None]
    ).astype(jnp.bfloat16)
    log_home = home_max + jnp.log(home_norm)
    grad_home = output_gradient.reshape(home_rows, pair_heads, groups, HEAD_SIZE).astype(
        jnp.float32
    )
    delta_home = jnp.sum(grad_home * attn_home.astype(jnp.float32), axis=-1)
    log_all, delta_all = (
        lax.all_gather(log_home, "dp", axis=0, tiled=True),
        lax.all_gather(delta_home, "dp", axis=0, tiled=True),
    )
    attention = attn_home.reshape(home_rows, pair_heads, group_width)
    log_blocks = log_all.reshape(block_count, block_rows, pair_heads, groups)
    delta_blocks = delta_all.reshape(block_count, block_rows, pair_heads, groups)

    def block_grad(totals, inputs):
        query_block, grad_block, places, query_doc, log_norm, row_delta = inputs
        allowed = admissible(places, query_doc)

        def compute():
            shifted = scores_of(query_block) - log_norm.transpose(2, 1, 0)[..., None]
            probs = jnp.where(allowed[None, None], jnp.exp(shifted), 0.0)
            value_grad = jnp.einsum(
                "gjpk,pjgd->kgd",
                probs.astype(jnp.bfloat16),
                grad_block,
                preferred_element_type=jnp.float32,
            )
            weight_grad = jnp.einsum(
                "pjgd,kgd->gjpk", grad_block, value_heads, preferred_element_type=jnp.float32
            )
            score_grad = (probs * (weight_grad - row_delta.transpose(2, 1, 0)[..., None])).astype(
                jnp.bfloat16
            )
            query_grad = (
                jnp.einsum(
                    "gjpk,kgd->pjgd", score_grad, key_heads, preferred_element_type=jnp.float32
                )
                * scale_factor
            )
            key_grad = (
                jnp.einsum(
                    "gjpk,pjgd->kgd", score_grad, query_block, preferred_element_type=jnp.float32
                )
                * scale_factor
            )
            return (query_grad.reshape(block_rows, pair_heads, group_width), key_grad, value_grad)

        query_grad, key_grad, value_grad = compute()
        return ((totals[0] + key_grad, totals[1] + value_grad), query_grad)

    zero_start = jnp.zeros((key_count, groups, HEAD_SIZE), jnp.float32)
    grad_inputs = (query_blocks, grad_blocks, place_blocks, doc_blocks, log_blocks, delta_blocks)
    (key_total, value_total), query_parts = lax.scan(
        block_grad, (zero_start, zero_start), grad_inputs
    )
    q_summed = lax.psum_scatter(
        query_parts.reshape(query_total, pair_heads, group_width).astype(jnp.bfloat16),
        "dp",
        scatter_dimension=0,
        tiled=True,
    )
    spread_key, spread_value = (
        lax.all_to_all(
            key_total.reshape(key_count, group_width).astype(jnp.bfloat16),
            "head",
            split_axis=0,
            concat_axis=1,
            tiled=True,
        ).astype(jnp.float32),
        lax.all_to_all(
            value_total.reshape(key_count, group_width).astype(jnp.bfloat16),
            "head",
            split_axis=0,
            concat_axis=1,
            tiled=True,
        ).astype(jnp.float32),
    )
    k_summed, v_summed = (
        lax.psum_scatter(
            spread_key.astype(jnp.bfloat16), "srv", scatter_dimension=0, tiled=True
        ).astype(jnp.float32),
        lax.psum_scatter(
            spread_value.astype(jnp.bfloat16), "srv", scatter_dimension=0, tiled=True
        ).astype(jnp.float32),
    )
    return (attention, q_summed, k_summed.astype(jnp.bfloat16), v_summed.astype(jnp.bfloat16))


def solution(mesh):
    placed = (
        P("dp", "srv", "head"),
        P(("dp", "head"), None),
        P(("dp", "head"), None),
        P("dp", "srv", "head"),
        P("dp"),
    )
    return jax.shard_map(
        local,
        mesh=mesh,
        in_specs=placed,
        out_specs=(
            P("dp", "srv", "head"),
            P("dp", "srv", "head"),
            P(("dp", "head", "srv"), None),
            P(("dp", "head", "srv"), None),
        ),
        check_vma=False,
    )
```

profile of v0, /device:TPU:2, one launch (start us, length us, event | category | flops | bytes accessed | tf_op | source)
XLA Modules:
  0.0 651.0 jit_solution(6897663471784736279)
XLA Ops:
  9.5 9.2 %all-to-all-start = ((bf16[80,8,128]{2,0,1:T(8,128)(2,1)}), bf16[80,8,128]{2,0,1:T(8,128)(2,1)S(1)}, u32[]{:S(2)}, u32[]{:S(2)}) async-start(bf16[80,8,128]{2,0,1:T(8,128)(2,1)} %copy_bitcast_fusion.3), calls=%async_computation | async-start | bytes 327680 | tf_op jit(solution)/shard_map/all_to_all | solution.py:16
  21.0 31.2 %all-gather.1 = s32[16,1,640]{2,1,0:T(1,128)S(1)} all-gather(s32[1,1,640]{2,1,0:T(1,128)S(1)} %reshape.364), channel_id=1, replica_groups=mesh['dp'=16,'head'=8,'srv'=4] {'dp'}, dimensions={0}, use_global_device_ids=true | all-gather | bytes 43520 | tf_op jit(solution)/shard_map/all_gather | solution.py:23
  52.8 33.4 %all-gather.5.cloned.1.call-done = bf16[2048,2,128]{2,0,1:T(8,128)(2,1)} async-done(((bf16[128,2,128]{2,0,1:T(8,128)(2,1)}), bf16[2048,2,128]{2,0,1:T(8,128)(2,1)}) %all-gather.5.cloned.1.call-update) | async-done | bytes 1048592 | tf_op jit(solution)/shard_map/all_gather | solution.py:29
  87.6 4.8 all-to-all-start.1
  92.4 7.6 %while.39 = (s32[]{:T(128)}, f32[4,512,2,1]{1,0,2,3:T(4,128)S(1)}, s32[4,512]{1,0:T(4,128)}, s32[640]{0:T(1024)S(1)}, s32[4,512]{1,0:T(4,128)S(1)}, /*index=5*/b...) while((s32[]{:T(128)}, f32[4,512,2,1]{1,0,2,3:T(4,128)S(1)}, ...), condition=%wide.region_2.3_spmd.clone, body=%wide.region_0.2_spmd.clone.sunk | while | flops 170720896 | bytes 1121917 | solution.py:64
  100.0 55.1 %pmax.7 = f32[2048,2,1]{0,1,2:T(2,128)} all-reduce(f32[2048,2,1]{0,1,2:T(2,128)S(1)} %reshape.354), channel_id=1, replica_groups=mesh['dp'=16,'head'=8,'srv'=4] {'dp'}, use_global_device_ids=true, to_apply=%region_3.4 | all-reduce | flops 4096 | bytes 32768 | tf_op jit(solution)/shard_map/pmax | solution.py:65
  155.1 22.3 %while.40 = (s32[]{:T(128)}, f32[4,512,2,128]{3,2,1,0:T(2,128)S(1)}, f32[4,512,2,1]{1,3,2,0:T(1,128)}, s32[4,512]{1,0:T(4,128)}, s32[640]{0:T(1024)S(1)}, /*inde...) while((s32[]{:T(128)}, ...), condition=%wide.region_6.7_spmd.clone, body=%wide.region_4.6_spmd.clone.sunk | while | flops 341769856 | bytes 8437397 | solution.py:89
  183.0 63.6 %reduce-scatter.8.cloned.1.call-done = f32[128,2]{1,0:T(8,128)} async-done(((f32[2048,2]{1,0:T(8,128)}), f32[128,2]{1,0:T(8,128)}) %reduce-scatter.8.cloned.1.call-update) | async-done | bytes 1040
  248.3 27.4 %all_gather.17 = f32[2048,2,1]{0,1,2:T(2,128)S(1)} all-gather(f32[128,2,1]{0,1,2:T(2,128)S(1)} %log_add_fusion), channel_id=1, replica_groups=mesh['dp'=16,'head'=8,'srv'=4] {'dp'}, dimensions={0}, use_global_device_ids=true | all-gather | bytes 17408 | tf_op jit(solution)/shard_map/all_gather | solution.py:106
  275.7 115.2 %all-reduce.10.cloned.1.call-done = f32[2048,2,128]{2,1,0:T(2,128)} async-done(((f32[2048,2,128]{2,1,0:T(2,128)}), f32[2048,2,128]{2,1,0:T(2,128)}) %all-reduce.10.cloned.1.call-update) | async-done | bytes 2097168
  392.6 35.8 %all-gather = f32[2048,2]{1,0:T(8,128)S(1)} all-gather(f32[128,2]{1,0:T(8,128)S(1)} %get-tuple-element.445), channel_id=2, replica_groups=mesh['dp'=16,'head'=8,'srv'=4] {'dp'}, dimensions={0}, use_global_device_ids=true | all-gather | bytes 17408 | tf_op jit(solution)/shard_map/all_gather | solution.py:107
  428.7 32.1 %all-gather.7.cloned.1.call-done = bf16[2048,2,128]{2,0,1:T(8,128)(2,1)} async-done(((bf16[128,2,128]{2,0,1:T(8,128)(2,1)}), bf16[2048,2,128]{2,0,1:T(8,128)(2,1)}) %all-gather.7.cloned.1.call-update) | async-done | bytes 1048592 | tf_op jit(solution)/shard_map/all_gather | solution.py:30
  460.8 37.4 %while.41 = (s32[]{:T(128)}, f32[640,1,128]{0,2,1:T(8,128)S(1)}, f32[640,1,128]{0,2,1:T(8,128)}, bf16[4,512,2,128]{3,1,2,0:T(8,128)(2,1)}, bf16[4,512,2,1,128]{4...) while((s32[]{:T(128)}, f32[640,1,128]{0,2,1:T(8,128)S(1)}, ...), condition=%wide.region_11.12_spmd.clone, body=%wide.region_10.11_spmd.clone.sunk | while | flops 846938752 | bytes 35077916 | solution.py:151
  465.0 3.6 fusion.122
  474.4 3.6 fusion.122
  483.7 3.6 fusion.122
  493.1 3.6 fusion.122
  499.0 4.9 all-to-all-start.2
  503.9 3.3 copy.77
  508.9 4.8 all-to-all-start.3
  513.7 5.0 all-to-all-done.3
  518.8 12.6 %fusion.72 = (bf16[24,1024]{1,0:T(8,128)(2,1)S(1)}, bf16[24,1024]{1,0:T(8,128)(2,1)S(1)}) fusion(bf16[80,1024]{1,0:T(8,128)(2,1)S(1)} %copy_bitcast_fusion.1, bf16[80,1024]{1,0:T(8,128)(2,1)S(1)} %copy_bitcast_fusion), kind=kCustom, calls=%all-reduce-scatter.2 | all-reduce-scatter fusion | flops 196609 | bytes 428032
  533.0 3.1 collective-permute-start.1
  539.6 103.4 %all-reduce.12.cloned.1.call-done = bf16[2048,2,128]{2,1,0:T(2,128)(2,1)} async-done(((bf16[2048,2,128]{2,1,0:T(2,128)(2,1)}), bf16[2048,2,128]{2,1,0:T(2,128)(2,1)}) %all-reduce.12.cloned.1.call-update) | async-done | bytes 1048592
  (173 shorter events, 76.1 us)
Async XLA Ops:
  7.2 1.6 copy-start
  7.2 85.2 %copy-start.3 = (s32[640]{0:T(1024)S(1)}, s32[640]{0:T(1024)}, u32[]{:S(2)}) copy-start(s32[640]{0:T(1024)} %param.15) | copy-start | bytes 7684
  7.2 79.1 %all-gather.5.cloned.1.call-start = ((), (), s32[]{:S(2)}) async-start(), calls=%async_computation.5 | async-start | bytes 1114112 | tf_op jit(solution)/shard_map/all_gather | solution.py:29
  9.5 78.1 %all-to-all-start = ((bf16[80,8,128]{2,0,1:T(8,128)(2,1)}), bf16[80,8,128]{2,0,1:T(8,128)(2,1)S(1)}, u32[]{:S(2)}, u32[]{:S(2)}) async-start(bf16[80,8,128]{2,0,1:T(8,128)(2,1)} %copy_bitcast_fusion.3), calls=%async_computation | async-start | bytes 327680 | tf_op jit(solution)/shard_map/all_to_all | solution.py:16
  87.6 67.6 %all-to-all-start.1 = ((bf16[80,8,128]{2,0,1:T(8,128)(2,1)}), bf16[80,8,128]{2,0,1:T(8,128)(2,1)}, u32[]{:S(2)}, u32[]{:S(2)}) async-start(bf16[80,8,128]{2,0,1:T(8,128)(2,1)} %copy_bitcast_fusion.2), calls=%async_computation.1 | async-start | bytes 327680 | tf_op jit(solution)/shard_map/all_to_all | solution.py:17
  92.4 154.2 %reduce-scatter.8.cloned.1.call-start = ((), (), s32[]{:S(2)}) async-start(), calls=%async_computation.7 | async-start | bytes 1114112
  177.4 2.2 copy-start.2
  177.4 2.9 copy-start.7
  179.6 211.3 %all-reduce.10.cloned.1.call-start = ((), (), s32[]{:S(2)}) async-start(), calls=%async_computation.8 | async-start | bytes 4194304
  180.3 280.5 %all-gather.7.cloned.1.call-start = ((), (), s32[]{:S(2)}) async-start(), calls=%async_computation.6 | async-start | bytes 1114112 | tf_op jit(solution)/shard_map/all_gather | solution.py:30
  461.3 3.2 copy-start.1
  465.0 3.6 copy-start.4
  470.7 3.2 copy-start.1
  474.4 3.6 copy-start.4
  480.0 3.2 copy-start.1
  483.7 3.6 copy-start.4
  489.4 3.2 copy-start.1
  493.1 3.6 copy-start.4
  498.2 9.0 %copy-start.6 = (f32[640,1,128]{0,2,1:T(8,128)S(1)}, f32[640,1,128]{0,2,1:T(8,128)}, u32[]{:S(2)}) copy-start(f32[640,1,128]{0,2,1:T(8,128)} %get-tuple-element.183) | copy-start | bytes 983044
  499.0 9.9 %all-to-all-start.2 = ((bf16[8,80,128]{2,1,0:T(8,128)(2,1)}), bf16[8,80,128]{2,1,0:T(8,128)(2,1)S(1)}, u32[]{:S(2)}, u32[]{:S(2)}) async-start(bf16[8,80,128]{2,1,0:T(8,128)(2,1)} %bitcast.15), calls=%async_computation.2 | async-start | bytes 327680 | tf_op jit(solution)/shard_map/all_to_all | solution.py:161
  503.9 139.1 %all-reduce.12.cloned.1.call-start = ((), (), s32[]{:S(2)}) async-start(), calls=%async_computation.9 | async-start | bytes 2097152
  508.9 9.8 %all-to-all-start.3 = ((bf16[8,80,128]{2,1,0:T(8,128)(2,1)}), bf16[8,80,128]{2,1,0:T(8,128)(2,1)S(1)}, u32[]{:S(2)}, u32[]{:S(2)}) async-start(bf16[8,80,128]{2,1,0:T(8,128)(2,1)} %bitcast.17), calls=%async_computation.3 | async-start | bytes 327680 | tf_op jit(solution)/shard_map/all_to_all | solution.py:168
  531.4 6.6 %collective-permute-start = (bf16[12,1024]{1,0:T(8,128)(2,1)S(1)}, bf16[12,1024]{1,0:T(8,128)(2,1)S(1)}, u32[]{:S(2)}, u32[]{:S(2)}) collective-permute-start(bf16[12,1024]{1,0:T(8,128)(2,1)S(1)} %slice.16), channel_id=1, source_target_pairs={{0,1},{1,2},{2,3},{4,5},{5,6},{6,7},{8,9},{9,10},{10,11},{12,13},{... | collective-permute-start | bytes 73736
  533.0 5.2 collective-permute-start.1
  (4 other events, 4.0 us)
Sparse Core Ops, SparseCore 0:
  10.7 75.5 all-gather.4
  179.7 66.8 reduce-scatter.7
  249.1 141.7 all-reduce.9
  393.6 67.1 all-gather.6
  507.3 135.5 all-reduce.11
where the time goes:
time: 653 us; the launch traced here: 651 us
  waiting for transfers between devices  354 us (54%)
  blocking collectives  162 us (25%)
  matrix products  42.8 us (7%)
  local copies, waits for them, and re-layouts  40.5 us (6%)
  starting transfers between devices  28.4 us (4%)
  between operations  15.3 us (2%)
  other arithmetic  7 us (1%)
    unnamed x10, waiting for transfers between devices  283 us
    pmax x1, blocking collectives, local(): row_max = lax.pmax(local_max.reshape(query_total, pair_heads, groups), 'dp')  55.1 us
    all_gather x1, blocking collectives, local(): lax.all_gather(delta_home, 'dp', axis=0, tiled=True)  35.8 us
    all_gather x1, waiting for transfers between devices, local(): lax.all_gather(queries, 'dp', axis=0, tiled=True)  33.4 us
    all_gather x1, waiting for transfers between devices, local(): lax.all_gather(output_gradient, 'dp', axis=0, tiled=True)  32.1 us
    all_gather x1, blocking collectives, local(): all_docs = lax.all_gather(doc_ids, 'dp', axis=0, tiled=True)  31.2 us
    all_gather x1, blocking collectives, local(): lax.all_gather(log_home, 'dp', axis=0, tiled=True)  27.4 us
    dot_general x4, matrix products, compute(): jnp.einsum('gjpk,pjgd->kgd', probs.astype(jnp.bfloat16), grad_block, pref...  14.3 us
  transfers between devices with their start and end apart: 11, of which 7 were waited for; matrix products, arithmetic and copies ran while one was open for 6% of the time, Pallas kernels for 0%

commit v1 on v0

--- a/solution.py
+++ b/solution.py
@@ -6,6 +6,28 @@
 
 HEAD_SIZE = 128
 NEGATIVE = -1e30
+
+
+def joined_along(blocks, dim):
+    blocks = jnp.moveaxis(blocks, 0, dim)
+    lengths = blocks.shape
+    return blocks.reshape(*lengths[:dim], lengths[dim] * lengths[dim + 1], *lengths[dim + 2 :])
+
+
+def collect(x, axis, dim):
+    size = lax.axis_size(axis)
+    pairs = [(i, (i + 1) % size) for i in range(size)]
+    back = [(b, a) for a, b in pairs]
+    lower, upper = ([], [])
+    for step in range(size - 1):
+        if step % 2 == 0:
+            lower.append(lax.ppermute(lower[-1] if lower else x, axis, pairs))
+        else:
+            upper.append(lax.ppermute(upper[-1] if upper else x, axis, back))
+    blocks = jnp.stack([*lower[::-1], x, *upper])
+    shift = lax.axis_index(axis) - len(lower)
+    blocks = blocks[(jnp.arange(size) - shift) % size]
+    return joined_along(blocks, dim)
 
 
 def local(queries, keys, values, output_gradient, doc_ids):
@@ -104,7 +126,7 @@
     delta_home = jnp.sum(grad_home * attn_home.astype(jnp.float32), axis=-1)
     log_all, delta_all = (
         lax.all_gather(log_home, "dp", axis=0, tiled=True),
-        lax.all_gather(delta_home, "dp", axis=0, tiled=True),
+        collect(delta_home, "dp", 0),
     )
     attention = attn_home.reshape(home_rows, pair_heads, group_width)
     log_blocks = log_all.reshape(block_count, block_rows, pair_heads, groups)

time: 653 us -> 677 us (1.037)
  starting transfers between devices: 28.4 us -> 77.6 us
  blocking collectives: 162 us -> 128 us
  waiting for transfers between devices: 354 us -> 362 us
    ppermute x0 -> x15, starting transfers between devices: none -> 49.3 us  [the longest x7 32.7 us: collect(): upper.append(lax.ppermute(upper[-1] if upper else x, axis, back))]
    all_gather x1 -> x0, blocking collectives: 35.8 us -> none  [local(): lax.all_gather(delta_home, 'dp', axis=0, tiled=True)]
    unnamed x10, waiting for transfers between devices: 283 us -> 312 us
    all_gather x1, waiting for transfers between devices: 32.1 us -> 3.58 us  [local(): lax.all_gather(output_gradient, 'dp', axis=0, tiled=True)]
    ppermute x0 -> x15, waiting for transfers between devices: none -> 6.87 us  [the longest x8 3.51 us: collect(): lower.append(lax.ppermute(lower[-1] if lower else x, axis, pairs))]
  transfers between devices with their start and end apart: 11 -> 26, of which waited for: 7 -> 9; matrix products, arithmetic and copies ran while one was open for 6% -> 5% of each run, Pallas kernels for 0% -> 0%
where the time goes in v1:
time: 677 us; the launch traced here: 675 us
  waiting for transfers between devices  362 us (53%)
  blocking collectives  128 us (19%)
  starting transfers between devices  77.6 us (11%)
  matrix products  42.9 us (6%)
  local copies, waits for them, and re-layouts  40.9 us (6%)
  between operations  15.5 us (2%)
  other arithmetic  7.02 us (1%)
    unnamed x10, waiting for transfers between devices  312 us
    pmax x1, blocking collectives, local(): row_max = lax.pmax(local_max.reshape(query_total, pair_heads, groups), 'dp')  55.1 us
    all_gather x1, waiting for transfers between devices, local(): lax.all_gather(queries, 'dp', axis=0, tiled=True)  33.4 us
    ppermute x7, starting transfers between devices, collect(): upper.append(lax.ppermute(upper[-1] if upper else x, axis, back))  32.7 us
    all_gather x1, blocking collectives, local(): all_docs = lax.all_gather(doc_ids, 'dp', axis=0, tiled=True)  31.2 us
    all_gather x1, blocking collectives, local(): lax.all_gather(log_home, 'dp', axis=0, tiled=True)  29.2 us
    ppermute x8, starting transfers between devices, collect(): lower.append(lax.ppermute(lower[-1] if lower else x, axis, pairs))  16.7 us
    dot_general x4, matrix products, compute(): jnp.einsum('gjpk,pjgd->kgd', probs.astype(jnp.bfloat16), grad_block, pref...  14.3 us
  transfers between devices with their start and end apart: 26, of which 9 were waited for; matrix products, arithmetic and copies ran while one was open for 5% of the time, Pallas kernels for 0%

profile of v1, /device:TPU:2, one launch (start us, length us, event | category | flops | bytes accessed | tf_op | source)
XLA Modules:
  0.0 674.6 jit_solution(462577911891509067)
XLA Ops:
  9.5 9.2 %all-to-all-start = ((bf16[80,8,128]{2,0,1:T(8,128)(2,1)}), bf16[80,8,128]{2,0,1:T(8,128)(2,1)S(1)}, u32[]{:S(2)}, u32[]{:S(2)}) async-start(bf16[80,8,128]{2,0,1:T(8,128)(2,1)} %copy_bitcast_fusion.3), calls=%async_computation | async-start | bytes 327680 | tf_op jit(solution)/shard_map/all_to_all | solution.py:38
  21.0 31.2 %all-gather = s32[16,1,640]{2,1,0:T(1,128)S(1)} all-gather(s32[1,1,640]{2,1,0:T(1,128)S(1)} %reshape.419), channel_id=1, replica_groups=mesh['dp'=16,'head'=8,'srv'=4] {'dp'}, dimensions={0}, use_global_device_ids=true | all-gather | bytes 43520 | tf_op jit(solution)/shard_map/all_gather | solution.py:45
  52.8 33.4 %all-gather.4.cloned.1.call-done = bf16[2048,2,128]{2,0,1:T(8,128)(2,1)} async-done(((bf16[128,2,128]{2,0,1:T(8,128)(2,1)}), bf16[2048,2,128]{2,0,1:T(8,128)(2,1)}) %all-gather.4.cloned.1.call-update) | async-done | bytes 1048592 | tf_op jit(solution)/shard_map/all_gather | solution.py:51
  87.6 4.8 all-to-all-start.1
  92.4 7.6 %while.39 = (s32[]{:T(128)}, f32[4,512,2,1]{1,0,2,3:T(4,128)S(1)}, s32[4,512]{1,0:T(4,128)}, s32[640]{0:T(1024)S(1)}, s32[4,512]{1,0:T(4,128)S(1)}, /*index=5*/b...) while((s32[]{:T(128)}, f32[4,512,2,1]{1,0,2,3:T(4,128)S(1)}, ...), condition=%wide.region_2.3_spmd.clone, body=%wide.region_0.2_spmd.clone.sunk | while | flops 170720896 | bytes 1121917 | solution.py:86
  100.0 55.1 %pmax.7 = f32[2048,2,1]{0,1,2:T(2,128)} all-reduce(f32[2048,2,1]{0,1,2:T(2,128)S(1)} %reshape.401), channel_id=1, replica_groups=mesh['dp'=16,'head'=8,'srv'=4] {'dp'}, use_global_device_ids=true, to_apply=%region_3.4 | all-reduce | flops 4096 | bytes 32768 | tf_op jit(solution)/shard_map/pmax | solution.py:87
  155.1 22.3 %while.40 = (s32[]{:T(128)}, f32[4,512,2,128]{3,2,1,0:T(2,128)S(1)}, f32[4,512,2,1]{1,3,2,0:T(1,128)}, s32[4,512]{1,0:T(4,128)}, s32[640]{0:T(1024)S(1)}, /*inde...) while((s32[]{:T(128)}, ...), condition=%wide.region_6.7_spmd.clone, body=%wide.region_4.6_spmd.clone.sunk | while | flops 341769856 | bytes 8437397 | solution.py:111
  182.4 64.3 %reduce-scatter.8.cloned.1.call-done = f32[128,2]{1,0:T(8,128)} async-done(((f32[2048,2]{1,0:T(8,128)}), f32[128,2]{1,0:T(8,128)}) %reduce-scatter.8.cloned.1.call-update) | async-done | bytes 1040
  247.7 143.4 %all-reduce.10.cloned.1.call-done = f32[2048,2,128]{2,1,0:T(2,128)} async-done(((f32[2048,2,128]{2,1,0:T(2,128)}), f32[2048,2,128]{2,1,0:T(2,128)}) %all-reduce.10.cloned.1.call-update) | async-done | bytes 2097168
  401.6 5.1 collective-permute-start.8
  408.6 5.1 collective-permute-start.9
  416.4 5.1 collective-permute-start.10
  423.5 5.1 collective-permute-start.11
  430.6 5.1 collective-permute-start.12
  438.4 5.1 collective-permute-start.13
  445.5 29.2 %all_gather.14 = f32[2048,2,1]{0,1,2:T(2,128)S(1)} all-gather(f32[128,2,1]{0,1,2:T(2,128)S(1)} %log_add_fusion), channel_id=1, replica_groups=mesh['dp'=16,'head'=8,'srv'=4] {'dp'}, dimensions={0}, use_global_device_ids=true | all-gather | bytes 17408 | tf_op jit(solution)/shard_map/all_gather | solution.py:128
  484.3 37.3 %while.41 = (s32[]{:T(128)}, f32[640,1,128]{0,2,1:T(8,128)S(1)}, f32[640,1,128]{0,2,1:T(8,128)}, bf16[4,512,2,128]{3,1,2,0:T(8,128)(2,1)}, bf16[4,512,2,1,128]{4...) while((s32[]{:T(128)}, f32[640,1,128]{0,2,1:T(8,128)S(1)}, ...), condition=%wide.region_11.12_spmd.clone, body=%wide.region_10.11_spmd.clone.sunk | while | flops 846938752 | bytes 35077916 | solution.py:173
  507.1 3.6 fusion.124
  516.5 3.6 fusion.124
  522.4 4.8 all-to-all-start.2
  532.2 4.8 all-to-all-start.3
  537.0 5.0 all-to-all-done.3
  542.1 12.7 %fusion.74 = (bf16[24,1024]{1,0:T(8,128)(2,1)S(1)}, bf16[24,1024]{1,0:T(8,128)(2,1)S(1)}) fusion(bf16[80,1024]{1,0:T(8,128)(2,1)S(1)} %copy_bitcast_fusion.1, bf16[80,1024]{1,0:T(8,128)(2,1)S(1)} %copy_bitcast_fusion), kind=kCustom, calls=%all-reduce-scatter.2 | all-reduce-scatter fusion | flops 196609 | bytes 428032
  563.0 103.6 %all-reduce.12.cloned.1.call-done = bf16[2048,2,128]{2,1,0:T(2,128)(2,1)} async-done(((bf16[2048,2,128]{2,1,0:T(2,128)(2,1)}), bf16[2048,2,128]{2,1,0:T(2,128)(2,1)}) %all-reduce.12.cloned.1.call-update) | async-done | bytes 1048592
  (221 shorter events, 119.0 us)
Async XLA Ops:
  7.2 79.1 %all-gather.4.cloned.1.call-start = ((), (), s32[]{:S(2)}) async-start(), calls=%async_computation.5 | async-start | bytes 1114112 | tf_op jit(solution)/shard_map/all_gather | solution.py:51
  9.5 78.1 %all-to-all-start = ((bf16[80,8,128]{2,0,1:T(8,128)(2,1)}), bf16[80,8,128]{2,0,1:T(8,128)(2,1)S(1)}, u32[]{:S(2)}, u32[]{:S(2)}) async-start(bf16[80,8,128]{2,0,1:T(8,128)(2,1)} %copy_bitcast_fusion.3), calls=%async_computation | async-start | bytes 327680 | tf_op jit(solution)/shard_map/all_to_all | solution.py:38
  87.6 67.6 %all-to-all-start.1 = ((bf16[80,8,128]{2,0,1:T(8,128)(2,1)}), bf16[80,8,128]{2,0,1:T(8,128)(2,1)}, u32[]{:S(2)}, u32[]{:S(2)}) async-start(bf16[80,8,128]{2,0,1:T(8,128)(2,1)} %copy_bitcast_fusion.2), calls=%async_computation.1 | async-start | bytes 327680 | tf_op jit(solution)/shard_map/all_to_all | solution.py:39
  92.4 154.3 %reduce-scatter.8.cloned.1.call-start = ((), (), s32[]{:S(2)}) async-start(), calls=%async_computation.7 | async-start | bytes 1114112
  179.7 211.5 %all-reduce.10.cloned.1.call-start = ((), (), s32[]{:S(2)}) async-start(), calls=%async_computation.8 | async-start | bytes 4194304
  180.4 303.9 %all-gather.6.cloned.1.call-start = ((), (), s32[]{:S(2)}) async-start(), calls=%async_computation.6 | async-start | bytes 1114112 | tf_op jit(solution)/shard_map/all_gather | solution.py:52
  392.9 6.7 collective-permute-start
  399.6 7.1 %collective-permute-start.1 = (f32[128,2,1]{0,1,2:T(2,128)S(1)}, f32[128,2,1]{0,1,2:T(2,128)S(1)}, u32[]{:S(2)}, u32[]{:S(2)}) collective-permute-start(f32[128,2,1]{0,1,2:T(2,128)S(1)} %collective-permute-done), channel_id=1, source_target_pairs={{0,32},{32,64},{64,96},{96,128},{128,160},{160,192},{192,224},{224... | collective-permute-start | bytes 3080 | tf_op jit(solution)/shard_map/ppermute | solution.py:24
  401.6 7.0 %collective-permute-start.8 = (f32[128,2,1]{0,1,2:T(2,128)S(1)}, f32[128,2,1]{0,1,2:T(2,128)S(1)}, u32[]{:S(2)}, u32[]{:S(2)}) collective-permute-start(f32[128,2,1]{0,1,2:T(2,128)S(1)} %bitcast.410), channel_id=1, source_target_pairs={{32,0},{64,32},{96,64},{128,96},{160,128},{192,160},{224,192},{256... | collective-permute-start | bytes 3080 | tf_op jit(solution)/shard_map/ppermute | solution.py:26
  406.7 7.1 %collective-permute-start.2 = (f32[128,2,1]{0,1,2:T(2,128)S(1)}, f32[128,2,1]{0,1,2:T(2,128)S(1)}, u32[]{:S(2)}, u32[]{:S(2)}) collective-permute-start(f32[128,2,1]{0,1,2:T(2,128)S(1)} %collective-permute-done.1), channel_id=1, source_target_pairs={{0,32},{32,64},{64,96},{96,128},{128,160},{160,192},{192,224},{224... | collective-permute-start | bytes 3080 | tf_op jit(solution)/shard_map/ppermute | solution.py:24
  408.6 7.8 %collective-permute-start.9 = (f32[128,2,1]{0,1,2:T(2,128)S(1)}, f32[128,2,1]{0,1,2:T(2,128)S(1)}, u32[]{:S(2)}, u32[]{:S(2)}) collective-permute-start(f32[128,2,1]{0,1,2:T(2,128)S(1)} %collective-permute-done.8), channel_id=1, source_target_pairs={{32,0},{64,32},{96,64},{128,96},{160,128},{192,160},{224,192},{256... | collective-permute-start | bytes 3080 | tf_op jit(solution)/shard_map/ppermute | solution.py:26
  413.8 7.8 %collective-permute-start.3 = (f32[128,2,1]{0,1,2:T(2,128)S(1)}, f32[128,2,1]{0,1,2:T(2,128)S(1)}, u32[]{:S(2)}, u32[]{:S(2)}) collective-permute-start(f32[128,2,1]{0,1,2:T(2,128)S(1)} %collective-permute-done.2), channel_id=1, source_target_pairs={{0,32},{32,64},{64,96},{96,128},{128,160},{160,192},{192,224},{224... | collective-permute-start | bytes 3080 | tf_op jit(solution)/shard_map/ppermute | solution.py:24
  416.4 7.1 %collective-permute-start.10 = (f32[128,2,1]{0,1,2:T(2,128)S(1)}, f32[128,2,1]{0,1,2:T(2,128)S(1)}, u32[]{:S(2)}, u32[]{:S(2)}) collective-permute-start(f32[128,2,1]{0,1,2:T(2,128)S(1)} %collective-permute-done.9), channel_id=1, source_target_pairs={{32,0},{64,32},{96,64},{128,96},{160,128},{192,160},{224,192},{256... | collective-permute-start | bytes 3080 | tf_op jit(solution)/shard_map/ppermute | solution.py:26
  421.5 7.1 %collective-permute-start.4 = (f32[128,2,1]{0,1,2:T(2,128)S(1)}, f32[128,2,1]{0,1,2:T(2,128)S(1)}, u32[]{:S(2)}, u32[]{:S(2)}) collective-permute-start(f32[128,2,1]{0,1,2:T(2,128)S(1)} %collective-permute-done.3), channel_id=1, source_target_pairs={{0,32},{32,64},{64,96},{96,128},{128,160},{160,192},{192,224},{224... | collective-permute-start | bytes 3080 | tf_op jit(solution)/shard_map/ppermute | solution.py:24
  423.5 7.1 %collective-permute-start.11 = (f32[128,2,1]{0,1,2:T(2,128)S(1)}, f32[128,2,1]{0,1,2:T(2,128)S(1)}, u32[]{:S(2)}, u32[]{:S(2)}) collective-permute-start(f32[128,2,1]{0,1,2:T(2,128)S(1)} %collective-permute-done.10), channel_id=1, source_target_pairs={{32,0},{64,32},{96,64},{128,96},{160,128},{192,160},{224,192},{256... | collective-permute-start | bytes 3080 | tf_op jit(solution)/shard_map/ppermute | solution.py:26
  428.6 7.1 %collective-permute-start.5 = (f32[128,2,1]{0,1,2:T(2,128)S(1)}, f32[128,2,1]{0,1,2:T(2,128)S(1)}, u32[]{:S(2)}, u32[]{:S(2)}) collective-permute-start(f32[128,2,1]{0,1,2:T(2,128)S(1)} %collective-permute-done.4), channel_id=1, source_target_pairs={{0,32},{32,64},{64,96},{96,128},{128,160},{160,192},{192,224},{224... | collective-permute-start | bytes 3080 | tf_op jit(solution)/shard_map/ppermute | solution.py:24
  430.6 7.8 %collective-permute-start.12 = (f32[128,2,1]{0,1,2:T(2,128)S(1)}, f32[128,2,1]{0,1,2:T(2,128)S(1)}, u32[]{:S(2)}, u32[]{:S(2)}) collective-permute-start(f32[128,2,1]{0,1,2:T(2,128)S(1)} %collective-permute-done.11), channel_id=1, source_target_pairs={{32,0},{64,32},{96,64},{128,96},{160,128},{192,160},{224,192},{256... | collective-permute-start | bytes 3080 | tf_op jit(solution)/shard_map/ppermute | solution.py:26
  435.8 7.8 %collective-permute-start.6 = (f32[128,2,1]{0,1,2:T(2,128)S(1)}, f32[128,2,1]{0,1,2:T(2,128)S(1)}, u32[]{:S(2)}, u32[]{:S(2)}) collective-permute-start(f32[128,2,1]{0,1,2:T(2,128)S(1)} %collective-permute-done.5), channel_id=1, source_target_pairs={{0,32},{32,64},{64,96},{96,128},{128,160},{160,192},{192,224},{224... | collective-permute-start | bytes 3080 | tf_op jit(solution)/shard_map/ppermute | solution.py:24
  438.4 36.2 %collective-permute-start.13 = (f32[128,2,1]{0,1,2:T(2,128)S(1)}, f32[128,2,1]{0,1,2:T(2,128)S(1)}, u32[]{:S(2)}, u32[]{:S(2)}) collective-permute-start(f32[128,2,1]{0,1,2:T(2,128)S(1)} %collective-permute-done.12), channel_id=1, source_target_pairs={{32,0},{64,32},{96,64},{128,96},{160,128},{192,160},{224,192},{256... | collective-permute-start | bytes 3080 | tf_op jit(solution)/shard_map/ppermute | solution.py:26
  443.5 33.0 %collective-permute-start.7 = (f32[128,2,1]{0,1,2:T(2,128)S(1)}, f32[128,2,1]{0,1,2:T(2,128)S(1)}, u32[]{:S(2)}, u32[]{:S(2)}) collective-permute-start(f32[128,2,1]{0,1,2:T(2,128)S(1)} %collective-permute-done.6), channel_id=1, source_target_pairs={{0,32},{32,64},{64,96},{96,128},{128,160},{160,192},{192,224},{224... | collective-permute-start | bytes 3080 | tf_op jit(solution)/shard_map/ppermute | solution.py:24
  522.4 9.8 %all-to-all-start.2 = ((bf16[8,80,128]{2,1,0:T(8,128)(2,1)}), bf16[8,80,128]{2,1,0:T(8,128)(2,1)S(1)}, u32[]{:S(2)}, u32[]{:S(2)}) async-start(bf16[8,80,128]{2,1,0:T(8,128)(2,1)} %bitcast.48), calls=%async_computation.2 | async-start | bytes 327680 | tf_op jit(solution)/shard_map/all_to_all | solution.py:183
  527.2 139.4 %all-reduce.12.cloned.1.call-start = ((), (), s32[]{:S(2)}) async-start(), calls=%async_computation.9 | async-start | bytes 2097152
  532.2 9.8 %all-to-all-start.3 = ((bf16[8,80,128]{2,1,0:T(8,128)(2,1)}), bf16[8,80,128]{2,1,0:T(8,128)(2,1)S(1)}, u32[]{:S(2)}, u32[]{:S(2)}) async-start(bf16[8,80,128]{2,1,0:T(8,128)(2,1)} %bitcast.50), calls=%async_computation.3 | async-start | bytes 327680 | tf_op jit(solution)/shard_map/all_to_all | solution.py:190
  554.8 6.6 collective-permute-start.15
  (19 other events, 353.4 us)
Sparse Core Ops, SparseCore 0:
  10.7 75.5 all-gather.3
  179.8 66.8 reduce-scatter.7
  249.1 141.9 all-reduce.9
  416.5 67.7 all-gather.5
  530.6 135.9 all-reduce.11
